TPU v7x, 32 devices: a whole 2x2x4 slice. The times are simulated.
32 devices in a mesh: chan: 4 (over z), row: 4 (over x, core), col: 2 (over y).
Axes of the slice: x: 2, y: 2, z: 4, core: 2. Of those that a mesh axis runs over, the one named last changes fastest.
Arguments:
- voltages: bfloat16 [4, 4096, 512], P(None, ('chan', 'row', 'col')), may hold values from -6 to 6
- anchor_u_cells: int32 [4, 1024, 1024], P('chan', 'row', 'col'), may hold values from 0 to 255
- anchor_v_cells: int32 [4, 1024, 1024], P('chan', 'row', 'col'), may hold values from 0 to 255
- tile_kernel_offsets: int32 [4, 1024, 1024], P('chan', 'row', 'col'), may hold values from 0 to 63
- kernel_u: float32 [8, 32], replicated, may hold values from -3 to 3
- kernel_v: float32 [8, 32], replicated, may hold values from -3 to 3
Outputs:
- uv_grid: float32 [4, 2, 256, 256], P('chan', None, ('row', 'col'))
Inputs may be any that keep to these rules, and one draw needn't show every extreme that they name: tile_kernel_offsets holds ku * 8 + kv.
All inputs are finite; a program needn't handle non-finite values.
Results may differ from a plain program's by a relative error of at most 0.0029.
Values may be sent and summed in bfloat16 or wider, within the bound.
A program may use at most 512 MiB of HBM per device.

v0:
```python
import functools

import jax
import jax.numpy as jnp
from jax import lax
from jax.experimental import pallas as pl
from jax.experimental.pallas import tpu as pltpu
from jax.sharding import PartitionSpec as P

TILE_SIDE = 4
PATCH = 8
KERNEL_STEPS = 8
GRID_SIDE = 256
STEP_ROWS = 32


def rolled_table(kernel):
    table = kernel.reshape(KERNEL_STEPS, PATCH, TILE_SIDE)
    rolled = jnp.stack([jnp.roll(table, shift, axis=1) for shift in range(PATCH)], axis=1)
    return rolled.transpose(3, 2, 0, 1).reshape(TILE_SIDE * PATCH, KERNEL_STEPS * PATCH)


def grid_kernel(scale, left_ref, cols_ref, au_ref, av_ref, off_ref, table_ref, out_ref, vis, spread_v, spread_u):
    tile_cols = cols_ref.shape[0] // TILE_SIDE
    kinds = KERNEL_STEPS * PATCH
    bands = GRID_SIDE // PATCH
    step = pl.program_id(0)

    def multiply(slot):
        out_ref[...] += lax.dot_general(
            spread_v[slot], spread_u[slot], (((1,), (1,)), ((), ())), preferred_element_type=jnp.float32
        )

    def place(slot_ref, anchor, pieces):
        row = lax.broadcasted_iota(jnp.int32, (2 * PATCH, tile_cols), 0)
        low = anchor & (PATCH - 1)
        band = ((anchor >> 3) + ((row & (PATCH - 1)) < low).astype(jnp.int32)) & (bands - 1)
        band = (band - (row >> 3)).astype(jnp.float32).astype(jnp.bfloat16)
        for block in range(bands // 2):
            hit = band == jnp.bfloat16(2 * block)
            for plane, index_k, piece in pieces:
                start = plane * GRID_SIDE + block * 2 * PATCH
                slot_ref[start : start + 2 * PATCH, index_k * tile_cols : (index_k + 1) * tile_cols] = jnp.where(
                    hit, piece, jnp.bfloat16(0)
                )

    def build(slot, s):
        av = av_ref[pl.ds(s, 1), :]
        au = au_ref[pl.ds(s, 1), :]
        off = off_ref[pl.ds(s, 1), :]
        kind = lax.broadcasted_iota(jnp.int32, (kinds, tile_cols), 0)
        pick_v = (kind == (off & (KERNEL_STEPS - 1)) * PATCH + (av & (PATCH - 1))).astype(jnp.float32)
        pick_u = (kind == (off >> 3) * PATCH + (au & (PATCH - 1))).astype(jnp.float32)
        pick = jnp.concatenate([pick_v, pick_u], axis=0).astype(jnp.bfloat16)
        chosen = jnp.dot(table_ref[...], pick, preferred_element_type=jnp.float32)
        span = TILE_SIDE * PATCH
        kern_v = chosen[:span] + chosen[span : 2 * span]
        kern_u = chosen[2 * span :]
        pieces = []
        for index_k in range(TILE_SIDE):
            for plane in range(2):
                total = None
                for index_l in range(TILE_SIDE):
                    base = (plane * TILE_SIDE + index_k) * STEP_ROWS
                    value = vis[pl.ds(base + s, 1), index_l * tile_cols : (index_l + 1) * tile_cols]
                    term = value * kern_v[index_l * PATCH : (index_l + 1) * PATCH]
                    total = term if total is None else total + term
                pieces.append((plane, index_k, jnp.concatenate([total, total], axis=0).astype(jnp.bfloat16)))
        place(spread_v.at[slot], av, pieces)
        pieces = []
        for index_k in range(TILE_SIDE):
            piece = kern_u[index_k * PATCH : (index_k + 1) * PATCH]
            pieces.append((0, index_k, jnp.concatenate([piece, piece], axis=0).astype(jnp.bfloat16)))
        place(spread_u.at[slot], au, pieces)

    @pl.when(step == 0)
    def _():
        out_ref[...] = jnp.zeros_like(out_ref)
        spread_v[1] = jnp.zeros(spread_v.shape[1:], spread_v.dtype)
        spread_u[1] = jnp.zeros(spread_u.shape[1:], spread_u.dtype)

    for index_l in range(TILE_SIDE):
        part = slice(index_l * tile_cols, (index_l + 1) * tile_cols)
        gram = lax.dot_general(
            left_ref[0], cols_ref[part], (((1,), (1,)), ((), ())), preferred_element_type=jnp.float32
        )
        vis[:, part] = (gram * scale).astype(jnp.bfloat16).astype(jnp.float32)

    def pair(index, carry):
        build(0, 2 * index)
        multiply(1)
        build(1, 2 * index + 1)
        multiply(0)
        return carry

    lax.fori_loop(0, STEP_ROWS // 2, pair, 0)

    @pl.when(step == pl.num_programs(0) - 1)
    def _():
        multiply(1)


def grid_tiles(left, cols, au, av, off, table, scale):
    steps, left_rows, width = left.shape
    tile_cols = au.shape[1]
    depth = TILE_SIDE * tile_cols
    whole = lambda i: (0, 0)
    return pl.pallas_call(
        functools.partial(grid_kernel, scale),
        grid=(steps,),
        in_specs=[
            pl.BlockSpec((1, left_rows, width), lambda i: (i, 0, 0)),
            pl.BlockSpec(cols.shape, whole),
            pl.BlockSpec((STEP_ROWS, tile_cols), lambda i: (i, 0)),
            pl.BlockSpec((STEP_ROWS, tile_cols), lambda i: (i, 0)),
            pl.BlockSpec((STEP_ROWS, tile_cols), lambda i: (i, 0)),
            pl.BlockSpec(table.shape, whole),
        ],
        out_specs=pl.BlockSpec((2 * GRID_SIDE, GRID_SIDE), whole),
        out_shape=jax.ShapeDtypeStruct((2 * GRID_SIDE, GRID_SIDE), jnp.float32),
        scratch_shapes=[
            pltpu.VMEM((left_rows, depth), jnp.float32),
            pltpu.VMEM((2, 2 * GRID_SIDE, depth), jnp.bfloat16),
            pltpu.VMEM((2, GRID_SIDE, depth), jnp.bfloat16),
        ],
        compiler_params=pltpu.CompilerParams(vmem_limit_bytes=48 * 1024 * 1024),
    )(left, cols, au, av, off, table)


def body(voltages, anchor_u_cells, anchor_v_cells, tile_kernel_offsets, kernel_u, kernel_v):
    samples = voltages.shape[2] // 2
    n_rows = lax.axis_size("row")
    n_cols = lax.axis_size("col")
    n_chan = lax.axis_size("chan")
    shard_depth = voltages.shape[1]
    turned = lax.all_to_all(voltages, "chan", split_axis=0, concat_axis=1, tiled=True)
    local_chan = turned.shape[0]
    width = 2 * samples
    spread = lax.all_gather(turned, ("row", "col"), axis=1, tiled=True)
    all_volts = spread.reshape(local_chan, n_rows * n_cols, n_chan, shard_depth, width)
    all_volts = all_volts.transpose(0, 2, 1, 3, 4).reshape(
        local_chan, n_rows * n_cols * n_chan * shard_depth, width
    )
    row_count = all_volts.shape[1] // n_rows
    col_count = all_volts.shape[1] // n_cols
    row_volts = lax.dynamic_slice_in_dim(all_volts, lax.axis_index("row") * row_count, row_count, 1)
    col_volts = lax.dynamic_slice_in_dim(all_volts, lax.axis_index("col") * col_count, col_count, 1)
    tile_rows = row_count // TILE_SIDE
    tile_cols = col_count // TILE_SIDE
    steps = tile_rows // STEP_ROWS
    rows = row_volts[0].reshape(steps, STEP_ROWS, TILE_SIDE, width).transpose(0, 2, 1, 3)
    rows = rows.reshape(steps, TILE_SIDE * STEP_ROWS, width)
    turned_rows = jnp.concatenate([rows[..., samples:], -rows[..., :samples]], axis=2)
    left = jnp.concatenate([rows, turned_rows], axis=1)
    cols = col_volts[0].reshape(tile_cols, TILE_SIDE, width).transpose(1, 0, 2).reshape(col_count, width)
    table_v = rolled_table(kernel_v)
    table_u = rolled_table(kernel_u)
    high_v = table_v.astype(jnp.bfloat16).astype(jnp.float32)
    none = jnp.zeros_like(table_v)
    table = jnp.concatenate(
        [
            jnp.concatenate([high_v, none], axis=1),
            jnp.concatenate([table_v - high_v, none], axis=1),
            jnp.concatenate([none, table_u], axis=1),
        ],
        axis=0,
    ).astype(jnp.bfloat16)
    gridded = grid_tiles(
        left, cols, anchor_u_cells[0], anchor_v_cells[0], tile_kernel_offsets[0], table, 1.0 / samples
    )
    folded = gridded.reshape(1, 2, GRID_SIDE, GRID_SIDE).transpose(0, 1, 3, 2)
    return lax.psum_scatter(folded, ("row", "col"), scatter_dimension=2, tiled=True)


def solution(mesh):
    in_specs = (
        P(None, ("chan", "row", "col"), None),
        P("chan", "row", "col"),
        P("chan", "row", "col"),
        P("chan", "row", "col"),
        P(),
        P(),
    )
    out_specs = P("chan", None, ("row", "col"), None)
    return jax.shard_map(body, mesh=mesh, in_specs=in_specs, out_specs=out_specs, check_vma=False)
```

profile of v0, /device:TPU:0, one launch (start us, length us, event | category | flops | bytes accessed | tf_op | source)
XLA Modules:
  0.0 351.1 jit_solution(15061631648600280575)
XLA Ops:
  6.5 20.9 %all_to_all.12 = bf16[4,128,512]{2,1,0:T(8,128)(2,1)} all-to-all(bf16[4,128,512]{2,1,0:T(8,128)(2,1)} %param.6), channel_id=1, replica_groups=mesh['chan'=4,'row'=4,'col'=2] {'chan'}, dimensions={0} | all-to-all | bytes 1048576 | tf_op jit(solution)/shard_map/all_to_all | solution.py:136
  27.5 0.0 reduce-scatter.2.cloned.1.call-start
  27.5 0.8 copy.94
  28.5 0.2 copy.109
  28.7 0.1 reshape.40
  28.8 0.8 copy.77
  29.8 0.1 copy.93
  29.9 0.1 reshape.38
  30.0 0.1 fusion.5.table_ref
  30.1 33.3 %all-gather.2.cloned.1.call-done = bf16[1,4096,512]{2,1,0:T(8,128)(2,1)} async-done(((bf16[1,512,512]{2,1,0:T(8,128)(2,1)}), bf16[1,4096,512]{2,1,0:T(8,128)(2,1)}) %all-gather.2.cloned.1.call-update) | async-done | bytes 4194320 | tf_op jit(solution)/shard_map/all_gather | solution.py:139
  63.5 2.6 copy.74
  66.1 1.9 copy-done.3
  68.0 0.1 constant_dynamic-slice_fusion.1
  68.1 0.3 reshape_squeeze.6
  68.4 0.2 copy.75
  68.7 1.1 fusion.6
  69.7 1.2 copy-done.4
  71.0 0.1 constant_dynamic-slice_fusion
  71.1 2.0 reshape_squeeze.7
  73.2 3.5 copy.76
  76.7 0.2 maximum_maximum_fusion.left_ref
  76.9 232.1 %shard_map.64 = f32[512,256]{1,0:T(8,128)S(1)} custom-call(bf16[8,256,512]{2,1,0:T(8,128)(2,1)S(1)} %maximum_maximum_fusion.left_ref, bf16[2048,512]{1,0:T(8,128)(2,1)} %bitcast.88, s32[256,512]{1,0:T(8,128)S(1)} %bitcast.81, s32[256,512]{1,0:T(8,128)S(1)} %bitcast.82, s32[256,512]{1,0:T(8,128)S(1)} %bitcast.83, bf16[96,128]{1,0:T(8,128)(2,1)S(1)} %fusion.5.table_ref), custom_call_target="tpu_custom_call" | custom-call | tf_op jit(solution)/shard_map/pallas_call | solution.py:108
  309.0 1.0 copy.110
  310.0 34.3 %reduce-scatter.2.cloned.1.call-done = f32[1,2,32,256]{3,2,1,0:T(8,128)} async-done(((f32[1,2,256,256]{3,2,1,0:T(8,128)}), f32[1,2,32,256]{3,2,1,0:T(8,128)}) %reduce-scatter.2.cloned.1.call-update) | async-done | bytes 65552 | tf_op jit(solution)/shard_map/reduce_scatter | solution.py:172
  (46 shorter events, 0.4 us)
Async XLA Ops:
  6.5 56.9 %all-gather.2.cloned.1.call-start = ((), (), s32[]{:S(2)}) async-start(), calls=%async_computation.2 | async-start | bytes 4718592 | tf_op jit(solution)/shard_map/all_gather | solution.py:139
  27.5 316.8 %reduce-scatter.2.cloned.1.call-start = ((), (), s32[]{:S(2)}) async-start(), calls=%async_computation.3 | async-start | bytes 589824 | tf_op jit(solution)/shard_map/reduce_scatter | solution.py:172
  66.1 1.9 copy-start.3
  68.4 2.6 copy-start.4
  73.2 3.5 copy-start.5
  73.2 3.5 copy-start.6
  73.2 3.7 %copy-start = (s32[1,256,512]{2,1,0:T(8,128)S(1)}, s32[1,256,512]{2,1,0:T(8,128)}, u32[]{:S(2)}) copy-start(s32[1,256,512]{2,1,0:T(8,128)} %param.7) | copy-start | bytes 1572868
  73.2 3.7 %copy-start.1 = (s32[1,256,512]{2,1,0:T(8,128)S(1)}, s32[1,256,512]{2,1,0:T(8,128)}, u32[]{:S(2)}) copy-start(s32[1,256,512]{2,1,0:T(8,128)} %param.8) | copy-start | bytes 1572868
  73.2 3.7 %copy-start.2 = (s32[1,256,512]{2,1,0:T(8,128)S(1)}, s32[1,256,512]{2,1,0:T(8,128)}, u32[]{:S(2)}) copy-start(s32[1,256,512]{2,1,0:T(8,128)} %param.9) | copy-start | bytes 1572868
Sparse Core Ops, SparseCore 0:
  27.6 35.8 all-gather.1
  310.1 34.1 reduce-scatter.1
where the time goes:
time: 351 us
  Pallas kernels  232 us (66%)
  waiting for transfers between devices  67.6 us (19%)
  blocking collectives  20.9 us (6%)
  local copies, waits for them, and re-layouts  15.2 us (4%)
  between operations  13.7 us (4%)
    pallas_call x1, Pallas kernels, grid_tiles(): pl.pallas_call(functools.partial(grid_kernel, scale), grid=(steps,), in_s...  232 us
    reduce_scatter x1, waiting for transfers between devices, body(): lax.psum_scatter(folded, ('row', 'col'), scatter_dimension=2, tiled=True)  34.3 us
    all_gather x1, waiting for transfers between devices, body(): spread = lax.all_gather(turned, ('row', 'col'), axis=1, tiled=True)  33.3 us
    all_to_all x1, blocking collectives, body(): lax.all_to_all(voltages, 'chan', split_axis=0, concat_axis=1, tiled=True)  20.9 us
  transfers between devices with their start and end apart: 2, of which 2 were waited for; matrix products, arithmetic and copies ran while one was open for 1% of the time, Pallas kernels for 0%

commit v1 on v0

--- a/solution.py
+++ b/solution.py
@@ -12,6 +12,7 @@
 KERNEL_STEPS = 8
 GRID_SIDE = 256
 STEP_ROWS = 32
+GROUP = 4
 
 
 def rolled_table(kernel):
@@ -20,18 +21,18 @@
     return rolled.transpose(3, 2, 0, 1).reshape(TILE_SIDE * PATCH, KERNEL_STEPS * PATCH)
 
 
-def grid_kernel(scale, left_ref, cols_ref, au_ref, av_ref, off_ref, table_ref, out_ref, vis, spread_v, spread_u):
+def grid_kernel(scale, left_ref, cols_ref, au_ref, av_ref, off_ref, table_ref, out_ref, vis, spread_v, spread_u, acc):
     tile_cols = cols_ref.shape[0] // TILE_SIDE
     kinds = KERNEL_STEPS * PATCH
     bands = GRID_SIDE // PATCH
     step = pl.program_id(0)
 
-    def multiply(slot):
-        out_ref[...] += lax.dot_general(
-            spread_v[slot], spread_u[slot], (((1,), (1,)), ((), ())), preferred_element_type=jnp.float32
+    def multiply():
+        acc[...] += lax.dot_general(
+            spread_v[...], spread_u[...], (((1,), (1,)), ((), ())), preferred_element_type=jnp.float32
         )
 
-    def place(slot_ref, anchor, pieces):
+    def place(slot_ref, base, anchor, pieces):
         row = lax.broadcasted_iota(jnp.int32, (2 * PATCH, tile_cols), 0)
         low = anchor & (PATCH - 1)
         band = ((anchor >> 3) + ((row & (PATCH - 1)) < low).astype(jnp.int32)) & (bands - 1)
@@ -40,11 +41,11 @@
             hit = band == jnp.bfloat16(2 * block)
             for plane, index_k, piece in pieces:
                 start = plane * GRID_SIDE + block * 2 * PATCH
-                slot_ref[start : start + 2 * PATCH, index_k * tile_cols : (index_k + 1) * tile_cols] = jnp.where(
+                slot_ref[start : start + 2 * PATCH, pl.ds(base + index_k * tile_cols, tile_cols)] = jnp.where(
                     hit, piece, jnp.bfloat16(0)
                 )
 
-    def build(slot, s):
+    def build(lane, s):
         av = av_ref[pl.ds(s, 1), :]
         au = au_ref[pl.ds(s, 1), :]
         off = off_ref[pl.ds(s, 1), :]
@@ -66,18 +67,16 @@
                     term = value * kern_v[index_l * PATCH : (index_l + 1) * PATCH]
                     total = term if total is None else total + term
                 pieces.append((plane, index_k, jnp.concatenate([total, total], axis=0).astype(jnp.bfloat16)))
-        place(spread_v.at[slot], av, pieces)
+        place(spread_v, lane, av, pieces)
         pieces = []
         for index_k in range(TILE_SIDE):
             piece = kern_u[index_k * PATCH : (index_k + 1) * PATCH]
             pieces.append((0, index_k, jnp.concatenate([piece, piece], axis=0).astype(jnp.bfloat16)))
-        place(spread_u.at[slot], au, pieces)
+        place(spread_u, lane, au, pieces)
 
     @pl.when(step == 0)
     def _():
-        out_ref[...] = jnp.zeros_like(out_ref)
-        spread_v[1] = jnp.zeros(spread_v.shape[1:], spread_v.dtype)
-        spread_u[1] = jnp.zeros(spread_u.shape[1:], spread_u.dtype)
+        acc[...] = jnp.zeros_like(acc)
 
     for index_l in range(TILE_SIDE):
         part = slice(index_l * tile_cols, (index_l + 1) * tile_cols)
@@ -86,18 +85,23 @@
         )
         vis[:, part] = (gram * scale).astype(jnp.bfloat16).astype(jnp.float32)
 
-    def pair(index, carry):
-        build(0, 2 * index)
-        multiply(1)
-        build(1, 2 * index + 1)
-        multiply(0)
+    depth = TILE_SIDE * tile_cols
+
+    def group(index, carry):
+        def one(j, carry):
+            build(pl.multiple_of(j * depth, depth), index * GROUP + j)
+            return carry
+
+        for j in range(GROUP):
+            build(j * depth, index * GROUP + j)
+        multiply()
         return carry
 
-    lax.fori_loop(0, STEP_ROWS // 2, pair, 0)
+    lax.fori_loop(0, STEP_ROWS // GROUP, group, 0)
 
     @pl.when(step == pl.num_programs(0) - 1)
     def _():
-        multiply(1)
+        out_ref[...] = acc[...]
 
 
 def grid_tiles(left, cols, au, av, off, table, scale):
@@ -120,8 +124,9 @@
         out_shape=jax.ShapeDtypeStruct((2 * GRID_SIDE, GRID_SIDE), jnp.float32),
         scratch_shapes=[
             pltpu.VMEM((left_rows, depth), jnp.float32),
-            pltpu.VMEM((2, 2 * GRID_SIDE, depth), jnp.bfloat16),
-            pltpu.VMEM((2, GRID_SIDE, depth), jnp.bfloat16),
+            pltpu.VMEM((2 * GRID_SIDE, GROUP * depth), jnp.bfloat16),
+            pltpu.VMEM((GRID_SIDE, GROUP * depth), jnp.bfloat16),
+            pltpu.VMEM((2 * GRID_SIDE, GRID_SIDE), jnp.float32),
         ],
         compiler_params=pltpu.CompilerParams(vmem_limit_bytes=48 * 1024 * 1024),
     )(left, cols, au, av, off, table)
@@ -155,7 +160,7 @@
     cols = col_volts[0].reshape(tile_cols, TILE_SIDE, width).transpose(1, 0, 2).reshape(col_count, width)
     table_v = rolled_table(kernel_v)
     table_u = rolled_table(kernel_u)
-    high_v = table_v.astype(jnp.bfloat16).astype(jnp.float32)
+    high_v = lax.reduce_precision(table_v, 8, 7)
     none = jnp.zeros_like(table_v)
     table = jnp.concatenate(
         [

time: 351 us -> 294 us (0.84)
  Pallas kernels: 232 us -> 175 us
    pallas_call x1, Pallas kernels: 232 us -> 175 us  [grid_tiles(): pl.pallas_call(functools.partial(grid_kernel, scale), grid=(steps,), in_s...]
where the time goes in v1:
time: 294 us
  Pallas kernels  175 us (60%)
  waiting for transfers between devices  67.6 us (23%)
  blocking collectives  20.9 us (7%)
  local copies, waits for them, and re-layouts  15.2 us (5%)
  between operations  13.7 us (5%)
    pallas_call x1, Pallas kernels, grid_tiles(): pl.pallas_call(functools.partial(grid_kernel, scale), grid=(steps,), in_s...  175 us
    reduce_scatter x1, waiting for transfers between devices, body(): lax.psum_scatter(folded, ('row', 'col'), scatter_dimension=2, tiled=True)  34.3 us
    all_gather x1, waiting for transfers between devices, body(): spread = lax.all_gather(turned, ('row', 'col'), axis=1, tiled=True)  33.3 us
    all_to_all x1, blocking collectives, body(): lax.all_to_all(voltages, 'chan', split_axis=0, concat_axis=1, tiled=True)  20.9 us
  transfers between devices with their start and end apart: 2, of which 2 were waited for; matrix products, arithmetic and copies ran while one was open for 1% of the time, Pallas kernels for 0%

profile of v1, /device:TPU:0, one launch (start us, length us, event | category | flops | bytes accessed | tf_op | source)
XLA Modules:
  0.0 294.1 jit_solution(17907576407517864846)
XLA Ops:
  6.5 20.9 %all_to_all.12 = bf16[4,128,512]{2,1,0:T(8,128)(2,1)} all-to-all(bf16[4,128,512]{2,1,0:T(8,128)(2,1)} %param.6), channel_id=1, replica_groups=mesh['chan'=4,'row'=4,'col'=2] {'chan'}, dimensions={0} | all-to-all | bytes 1048576 | tf_op jit(solution)/shard_map/all_to_all | solution.py:141
  27.5 0.0 reduce-scatter.2.cloned.1.call-start
  27.5 0.8 copy.94
  28.5 0.2 copy.109
  28.7 0.1 reshape.40
  28.8 0.8 copy.77
  29.8 0.1 copy.93
  29.9 0.1 reshape.38
  30.0 0.1 fusion.5.table_ref
  30.1 33.3 %all-gather.2.cloned.1.call-done = bf16[1,4096,512]{2,1,0:T(8,128)(2,1)} async-done(((bf16[1,512,512]{2,1,0:T(8,128)(2,1)}), bf16[1,4096,512]{2,1,0:T(8,128)(2,1)}) %all-gather.2.cloned.1.call-update) | async-done | bytes 4194320 | tf_op jit(solution)/shard_map/all_gather | solution.py:144
  63.5 2.6 copy.74
  66.1 1.9 copy-done.3
  68.0 0.1 constant_dynamic-slice_fusion.1
  68.1 0.3 reshape_squeeze.6
  68.4 0.2 copy.75
  68.7 1.1 fusion.7
  69.7 1.2 copy-done.4
  71.0 0.1 constant_dynamic-slice_fusion
  71.1 2.0 reshape_squeeze.7
  73.2 3.5 %copy.76 = bf16[4,512,512]{2,1,0:T(8,128)(2,1)} copy(bf16[4,512,512]{2,0,1:T(4,128)(2,1)} %bitcast.89) | data formatting | bytes 4194304 | tf_op jit(solution)/shard_map/transpose | solution.py:160
  76.7 0.2 maximum_maximum_fusion.left_ref
  76.9 175.1 %shard_map.64 = f32[512,256]{1,0:T(8,128)S(1)} custom-call(bf16[8,256,512]{2,1,0:T(8,128)(2,1)S(1)} %maximum_maximum_fusion.left_ref, bf16[2048,512]{1,0:T(8,128)(2,1)} %bitcast.88, s32[256,512]{1,0:T(8,128)S(1)} %bitcast.81, s32[256,512]{1,0:T(8,128)S(1)} %bitcast.82, s32[256,512]{1,0:T(8,128)S(1)} %bitcast.83, bf16[96,128]{1,0:T(8,128)(2,1)S(1)} %fusion.5.table_ref), custom_call_target="tpu_custom_call" | custom-call | tf_op jit(solution)/shard_map/pallas_call | solution.py:112
  252.0 1.0 copy.110
  253.0 34.3 %reduce-scatter.2.cloned.1.call-done = f32[1,2,32,256]{3,2,1,0:T(8,128)} async-done(((f32[1,2,256,256]{3,2,1,0:T(8,128)}), f32[1,2,32,256]{3,2,1,0:T(8,128)}) %reduce-scatter.2.cloned.1.call-update) | async-done | bytes 65552 | tf_op jit(solution)/shard_map/reduce_scatter | solution.py:177
  (46 shorter events, 0.4 us)
Async XLA Ops:
  6.5 56.9 %all-gather.2.cloned.1.call-start = ((), (), s32[]{:S(2)}) async-start(), calls=%async_computation.2 | async-start | bytes 4718592 | tf_op jit(solution)/shard_map/all_gather | solution.py:144
  27.5 259.8 %reduce-scatter.2.cloned.1.call-start = ((), (), s32[]{:S(2)}) async-start(), calls=%async_computation.3 | async-start | bytes 589824 | tf_op jit(solution)/shard_map/reduce_scatter | solution.py:177
  66.1 1.9 copy-start.3
  68.4 2.6 copy-start.4
  73.2 3.5 %copy-start.5 = (bf16[8,128,256]{2,1,0:T(8,128)(2,1)S(1)}, bf16[8,128,256]{2,1,0:T(8,128)(2,1)}, u32[]{:S(2)}) copy-start(bf16[8,128,256]{2,1,0:T(8,128)(2,1)} %get-tuple-element.5) | copy-start | bytes 1572868
  73.2 3.5 %copy-start.6 = (bf16[8,128,256]{2,1,0:T(8,128)(2,1)S(1)}, bf16[8,128,256]{2,1,0:T(8,128)(2,1)}, u32[]{:S(2)}) copy-start(bf16[8,128,256]{2,1,0:T(8,128)(2,1)} %get-tuple-element.6) | copy-start | bytes 1572868
  73.2 3.7 %copy-start = (s32[1,256,512]{2,1,0:T(8,128)S(1)}, s32[1,256,512]{2,1,0:T(8,128)}, u32[]{:S(2)}) copy-start(s32[1,256,512]{2,1,0:T(8,128)} %param.7) | copy-start | bytes 1572868
  73.2 3.7 %copy-start.1 = (s32[1,256,512]{2,1,0:T(8,128)S(1)}, s32[1,256,512]{2,1,0:T(8,128)}, u32[]{:S(2)}) copy-start(s32[1,256,512]{2,1,0:T(8,128)} %param.8) | copy-start | bytes 1572868
  73.2 3.7 %copy-start.2 = (s32[1,256,512]{2,1,0:T(8,128)S(1)}, s32[1,256,512]{2,1,0:T(8,128)}, u32[]{:S(2)}) copy-start(s32[1,256,512]{2,1,0:T(8,128)} %param.9) | copy-start | bytes 1572868
Sparse Core Ops, SparseCore 0:
  27.6 35.8 all-gather.1
  253.1 34.1 reduce-scatter.1

commit v2 on v1

--- a/solution.py
+++ b/solution.py
@@ -12,7 +12,7 @@
 KERNEL_STEPS = 8
 GRID_SIDE = 256
 STEP_ROWS = 32
-GROUP = 4
+GROUP = 8
 
 
 def rolled_table(kernel):
@@ -130,6 +130,62 @@
         ],
         compiler_params=pltpu.CompilerParams(vmem_limit_bytes=48 * 1024 * 1024),
     )(left, cols, au, av, off, table)
+
+
+def scatter_kernel(n_rows, n_cols, parts_ref, out_ref, landed, send_sems, recv_sems):
+    peers = n_rows * n_cols
+    band = out_ref.shape[2]
+    me = lax.axis_index("row") * n_cols + lax.axis_index("col")
+    barrier = pltpu.get_barrier_semaphore()
+
+    def place_of(offset):
+        peer = lax.rem(me + offset, peers)
+        return peer, {"row": peer // n_cols, "col": lax.rem(peer, n_cols)}
+
+    for offset in range(1, peers):
+        pl.semaphore_signal(barrier, inc=1, device_id=place_of(offset)[1], device_id_type=pl.DeviceIdType.MESH)
+    pl.semaphore_wait(barrier, peers - 1)
+    copies = []
+    for offset in range(1, peers):
+        peer, place = place_of(offset)
+        copy = pltpu.make_async_remote_copy(
+            src_ref=parts_ref.at[:, :, pl.ds(pl.multiple_of(peer * band, band), band), :],
+            dst_ref=landed.at[offset - 1],
+            send_sem=send_sems.at[offset - 1],
+            recv_sem=recv_sems.at[offset - 1],
+            device_id=place,
+            device_id_type=pl.DeviceIdType.MESH,
+        )
+        copy.start()
+        copies.append(copy)
+    total = parts_ref[:, :, pl.ds(pl.multiple_of(me * band, band), band), :]
+    for index, copy in enumerate(copies):
+        copy.wait_recv()
+        total = total + landed[index]
+    out_ref[...] = total
+    for copy in copies:
+        copy.wait_send()
+
+
+def scatter_sum(parts):
+    n_rows = lax.axis_size("row")
+    n_cols = lax.axis_size("col")
+    peers = n_rows * n_cols
+    shape = (parts.shape[0], parts.shape[1], parts.shape[2] // peers, parts.shape[3])
+    return pl.pallas_call(
+        functools.partial(scatter_kernel, n_rows, n_cols),
+        in_specs=[pl.BlockSpec(memory_space=pltpu.VMEM)],
+        out_specs=pl.BlockSpec(memory_space=pltpu.VMEM),
+        out_shape=jax.ShapeDtypeStruct(shape, jnp.float32),
+        scratch_shapes=[
+            pltpu.VMEM((peers - 1,) + shape, jnp.float32),
+            pltpu.SemaphoreType.DMA((peers - 1,)),
+            pltpu.SemaphoreType.DMA((peers - 1,)),
+        ],
+        compiler_params=pltpu.CompilerParams(
+            collective_id=0, has_side_effects=True, vmem_limit_bytes=16 * 1024 * 1024
+        ),
+    )(parts)
 
 
 def body(voltages, anchor_u_cells, anchor_v_cells, tile_kernel_offsets, kernel_u, kernel_v):
@@ -174,7 +230,7 @@
         left, cols, anchor_u_cells[0], anchor_v_cells[0], tile_kernel_offsets[0], table, 1.0 / samples
     )
     folded = gridded.reshape(1, 2, GRID_SIDE, GRID_SIDE).transpose(0, 1, 3, 2)
-    return lax.psum_scatter(folded, ("row", "col"), scatter_dimension=2, tiled=True)
+    return scatter_sum(folded)
 
 
 def solution(mesh):

time: 294 us -> 267 us (0.908)
  waiting for transfers between devices: 67.6 us -> 33.4 us
  Pallas kernels: 175 us -> 182 us
    reduce_scatter x1 -> x0, waiting for transfers between devices: 34.3 us -> none  [body(): lax.psum_scatter(folded, ('row', 'col'), scatter_dimension=2, tiled=True)]
    pallas_call x0 -> x1, Pallas kernels: none -> 9.81 us  [scatter_sum(): pl.pallas_call(functools.partial(scatter_kernel, n_rows, n_cols), in_spec...]
    pallas_call x1, Pallas kernels: 175 us -> 172 us  [grid_tiles(): pl.pallas_call(functools.partial(grid_kernel, scale), grid=(steps,), in_s...]
  transfers between devices with their start and end apart: 2 -> 1, of which waited for: 2 -> 1; matrix products, arithmetic and copies ran while one was open for 1% -> 1% of each run, Pallas kernels for 0% -> 0%
where the time goes in v2:
time: 267 us; the launch traced here: 266 us
  Pallas kernels  182 us (68%)
  waiting for transfers between devices  33.4 us (13%)
  blocking collectives  20.9 us (8%)
  local copies, waits for them, and re-layouts  15 us (6%)
  between operations  13.7 us (5%)
    pallas_call x1, Pallas kernels, grid_tiles(): pl.pallas_call(functools.partial(grid_kernel, scale), grid=(steps,), in_s...  172 us
    all_gather x1, waiting for transfers between devices, body(): spread = lax.all_gather(turned, ('row', 'col'), axis=1, tiled=True)  33.4 us
    all_to_all x1, blocking collectives, body(): lax.all_to_all(voltages, 'chan', split_axis=0, concat_axis=1, tiled=True)  20.9 us
    pallas_call x1, Pallas kernels, scatter_sum(): pl.pallas_call(functools.partial(scatter_kernel, n_rows, n_cols), in_spec...  9.81 us
    unnamed x19, local copies, waits for them, and re-layouts  5.38 us
  transfers between devices with their start and end apart: 1, of which 1 were waited for; matrix products, arithmetic and copies ran while one was open for 1% of the time, Pallas kernels for 0%

profile of v2, /device:TPU:0, one launch (start us, length us, event | category | flops | bytes accessed | tf_op | source)
XLA Modules:
  0.0 266.3 jit_solution(5711028421403903755)
XLA Ops:
  6.5 20.9 %all_to_all.12 = bf16[4,128,512]{2,1,0:T(8,128)(2,1)} all-to-all(bf16[4,128,512]{2,1,0:T(8,128)(2,1)} %param.6), channel_id=1, replica_groups=mesh['chan'=4,'row'=4,'col'=2] {'chan'}, dimensions={0} | all-to-all | bytes 1048576 | tf_op jit(solution)/shard_map/all_to_all | solution.py:197
  27.5 0.8 copy.93
  28.5 0.2 copy.108
  28.7 0.1 reshape.40
  28.8 0.8 copy.76
  29.7 0.1 copy.92
  29.9 0.1 reshape.38
  30.0 0.1 fusion.5.table_ref
  30.1 33.4 %all-gather.2.cloned.1.call-done = bf16[1,4096,512]{2,1,0:T(8,128)(2,1)} async-done(((bf16[1,512,512]{2,1,0:T(8,128)(2,1)}), bf16[1,4096,512]{2,1,0:T(8,128)(2,1)}) %all-gather.2.cloned.1.call-update) | async-done | bytes 4194320 | tf_op jit(solution)/shard_map/all_gather | solution.py:200
  63.5 2.6 copy.73
  66.1 1.9 copy-done.3
  68.0 0.1 constant_dynamic-slice_fusion.1
  68.1 0.3 reshape_squeeze.6
  68.4 0.2 copy.74
  68.7 1.1 fusion.7
  69.7 1.2 copy-done.4
  71.0 0.1 constant_dynamic-slice_fusion
  71.1 2.0 reshape_squeeze.7
  73.2 3.5 %copy.75 = bf16[4,512,512]{2,1,0:T(8,128)(2,1)} copy(bf16[4,512,512]{2,0,1:T(4,128)(2,1)} %bitcast.90) | data formatting | bytes 4194304 | tf_op jit(solution)/shard_map/transpose | solution.py:216
  76.7 0.2 maximum_maximum_fusion.left_ref
  76.9 171.9 %shard_map.64 = f32[512,256]{1,0:T(8,128)S(1)} custom-call(bf16[8,256,512]{2,1,0:T(8,128)(2,1)S(1)} %maximum_maximum_fusion.left_ref, bf16[2048,512]{1,0:T(8,128)(2,1)} %bitcast.89, s32[256,512]{1,0:T(8,128)S(1)} %bitcast.82, s32[256,512]{1,0:T(8,128)S(1)} %bitcast.83, s32[256,512]{1,0:T(8,128)S(1)} %bitcast.84, bf16[96,128]{1,0:T(8,128)(2,1)S(1)} %fusion.5.table_ref), custom_call_target="tpu_custom_call" | custom-call | tf_op jit(solution)/shard_map/pallas_call | solution.py:112
  248.8 0.2 copy.109
  249.0 9.8 %shard_map.65 = f32[1,2,32,256]{3,2,1,0:T(8,128)S(1)} custom-call(f32[1,2,256,256]{3,2,1,0:T(8,128)S(1)} %bitcast.81), custom_call_target="tpu_custom_call" | custom-call | tf_op jit(solution)/shard_map/pallas_call | solution.py:175
  258.9 0.6 copy.139
  (45 shorter events, 0.3 us)
Async XLA Ops:
  6.5 56.9 %all-gather.2.cloned.1.call-start = ((), (), s32[]{:S(2)}) async-start(), calls=%async_computation.1 | async-start | bytes 4718592 | tf_op jit(solution)/shard_map/all_gather | solution.py:200
  66.1 1.9 copy-start.3
  68.4 2.6 copy-start.4
  73.2 3.5 %copy-start.5 = (bf16[8,128,256]{2,1,0:T(8,128)(2,1)S(1)}, bf16[8,128,256]{2,1,0:T(8,128)(2,1)}, u32[]{:S(2)}) copy-start(bf16[8,128,256]{2,1,0:T(8,128)(2,1)} %get-tuple-element.5) | copy-start | bytes 1572868
  73.2 3.5 %copy-start.6 = (bf16[8,128,256]{2,1,0:T(8,128)(2,1)S(1)}, bf16[8,128,256]{2,1,0:T(8,128)(2,1)}, u32[]{:S(2)}) copy-start(bf16[8,128,256]{2,1,0:T(8,128)(2,1)} %get-tuple-element.6) | copy-start | bytes 1572868
  73.2 3.7 %copy-start = (s32[1,256,512]{2,1,0:T(8,128)S(1)}, s32[1,256,512]{2,1,0:T(8,128)}, u32[]{:S(2)}) copy-start(s32[1,256,512]{2,1,0:T(8,128)} %param.7) | copy-start | bytes 1572868
  73.2 3.7 %copy-start.1 = (s32[1,256,512]{2,1,0:T(8,128)S(1)}, s32[1,256,512]{2,1,0:T(8,128)}, u32[]{:S(2)}) copy-start(s32[1,256,512]{2,1,0:T(8,128)} %param.8) | copy-start | bytes 1572868
  73.2 3.7 %copy-start.2 = (s32[1,256,512]{2,1,0:T(8,128)S(1)}, s32[1,256,512]{2,1,0:T(8,128)}, u32[]{:S(2)}) copy-start(s32[1,256,512]{2,1,0:T(8,128)} %param.9) | copy-start | bytes 1572868
Sparse Core Ops, SparseCore 0:
  27.6 35.8 all-gather.1

commit v3 on v2

--- a/solution.py
+++ b/solution.py
@@ -188,6 +188,94 @@
     )(parts)
 
 
+def gather_kernel(n_rows, n_cols, own_ref, cols_ref, rows_ref, local_sems, send_sems, recv_sems):
+    peers = n_rows * n_cols
+    deep_cols = cols_ref.shape[0]
+    deep_rows = rows_ref.shape[0]
+    row = lax.axis_index("row")
+    col = lax.axis_index("col")
+    me = row * n_cols + col
+    barrier = pltpu.get_barrier_semaphore()
+
+    def send(index, src, dst, place_row, place_col):
+        copy = pltpu.make_async_remote_copy(
+            src_ref=src,
+            dst_ref=dst,
+            send_sem=send_sems.at[index],
+            recv_sem=recv_sems.at[index],
+            device_id={"row": place_row, "col": place_col},
+            device_id_type=pl.DeviceIdType.MESH,
+        )
+        copy.start()
+        return copy
+
+    steps = [(dr, dc) for dr in range(n_rows) for dc in range(n_cols) if dr or dc]
+    for dr, dc in steps:
+        place = {"row": lax.rem(row + dr, n_rows), "col": lax.rem(col + dc, n_cols)}
+        pl.semaphore_signal(barrier, inc=1, device_id=place, device_id_type=pl.DeviceIdType.MESH)
+    pl.semaphore_wait(barrier, peers - 1)
+    twin = row + 1 - 2 * lax.rem(row, 2)
+    keep_cols = pltpu.make_async_copy(
+        own_ref.at[pl.ds(col * deep_cols, deep_cols)], cols_ref.at[:, me], local_sems.at[0]
+    )
+    keep_rows = pltpu.make_async_copy(
+        own_ref.at[pl.ds(row * deep_rows, deep_rows)], rows_ref.at[:, me], local_sems.at[1]
+    )
+    keep_cols.start()
+    keep_rows.start()
+    first = []
+    for dr, dc in steps:
+        if dr % 2 == 0:
+            to_row, to_col = lax.rem(row + dr, n_rows), lax.rem(col + dc, n_cols)
+            src = own_ref.at[pl.ds(to_col * deep_cols, deep_cols)]
+            first.append((dr, dc, send(len(first), src, cols_ref.at[:, me], to_row, to_col)))
+    count = len(first)
+    rest = [send(count, own_ref.at[pl.ds(col * deep_cols, deep_cols)], cols_ref.at[:, me], twin, col)]
+    count += 1
+    for dr, dc in steps:
+        to_row, to_col = lax.rem(row + dr, n_rows), lax.rem(col + dc, n_cols)
+        src = own_ref.at[pl.ds(to_row * deep_rows, deep_rows)]
+        rest.append(send(count, src, rows_ref.at[:, me], to_row, to_col))
+        count += 1
+    for dr, dc, copy in first:
+        copy.wait_recv()
+        origin = lax.rem(row - dr + n_rows, n_rows) * n_cols + lax.rem(col - dc + n_cols, n_cols)
+        rest.append(send(count, cols_ref.at[:, origin], cols_ref.at[:, origin], twin, col))
+        count += 1
+    for copy in rest:
+        copy.wait_recv()
+    for _, _, copy in first:
+        copy.wait_send()
+    for copy in rest:
+        copy.wait_send()
+    keep_cols.wait()
+    keep_rows.wait()
+
+
+def gather_sides(own):
+    n_rows = lax.axis_size("row")
+    n_cols = lax.axis_size("col")
+    n_chan, shard_depth, width = own.shape
+    peers = n_rows * n_cols
+    copies = peers // 2 - 1 + 1 + peers - 1 + peers // 2 - 1
+    anywhere = pl.BlockSpec(memory_space=pl.ANY)
+    return pl.pallas_call(
+        functools.partial(gather_kernel, n_rows, n_cols),
+        in_specs=[anywhere],
+        out_specs=[anywhere, anywhere],
+        out_shape=[
+            jax.ShapeDtypeStruct((n_chan // n_cols, peers, shard_depth, width), own.dtype),
+            jax.ShapeDtypeStruct((n_chan // n_rows, peers, shard_depth, width), own.dtype),
+        ],
+        scratch_shapes=[
+            pltpu.SemaphoreType.DMA((2,)),
+            pltpu.SemaphoreType.DMA((copies,)),
+            pltpu.SemaphoreType.DMA((copies,)),
+        ],
+        compiler_params=pltpu.CompilerParams(collective_id=1, has_side_effects=True),
+    )(own)
+
+
 def body(voltages, anchor_u_cells, anchor_v_cells, tile_kernel_offsets, kernel_u, kernel_v):
     samples = voltages.shape[2] // 2
     n_rows = lax.axis_size("row")
@@ -195,17 +283,12 @@
     n_chan = lax.axis_size("chan")
     shard_depth = voltages.shape[1]
     turned = lax.all_to_all(voltages, "chan", split_axis=0, concat_axis=1, tiled=True)
-    local_chan = turned.shape[0]
     width = 2 * samples
-    spread = lax.all_gather(turned, ("row", "col"), axis=1, tiled=True)
-    all_volts = spread.reshape(local_chan, n_rows * n_cols, n_chan, shard_depth, width)
-    all_volts = all_volts.transpose(0, 2, 1, 3, 4).reshape(
-        local_chan, n_rows * n_cols * n_chan * shard_depth, width
-    )
-    row_count = all_volts.shape[1] // n_rows
-    col_count = all_volts.shape[1] // n_cols
-    row_volts = lax.dynamic_slice_in_dim(all_volts, lax.axis_index("row") * row_count, row_count, 1)
-    col_volts = lax.dynamic_slice_in_dim(all_volts, lax.axis_index("col") * col_count, col_count, 1)
+    cols_side, rows_side = gather_sides(turned.reshape(n_chan, shard_depth, width))
+    row_count = n_chan * shard_depth * n_cols
+    col_count = n_chan * shard_depth * n_rows
+    row_volts = rows_side.reshape(1, row_count, width)
+    col_volts = cols_side.reshape(1, col_count, width)
     tile_rows = row_count // TILE_SIDE
     tile_cols = col_count // TILE_SIDE
     steps = tile_rows // STEP_ROWS

time: 267 us -> 239 us (0.90)
  Pallas kernels: 182 us -> 208 us
  waiting for transfers between devices: 33.4 us -> 11.9 us
  blocking collectives: 20.9 us -> 0 us
  between operations: 13.7 us -> 0.3 us
  starting transfers between devices: 0.01 us -> 6.32 us
  local copies, waits for them, and re-layouts: 15 us -> 10.8 us
    all_gather x1 -> x0, waiting for transfers between devices: 33.4 us -> none  [body(): spread = lax.all_gather(turned, ('row', 'col'), axis=1, tiled=True)]
    pallas_call x0 -> x1, Pallas kernels: none -> 26.1 us  [gather_sides(): pl.pallas_call(functools.partial(gather_kernel, n_rows, n_cols), in_specs...]
    all_to_all x1 -> x0, blocking collectives: 20.9 us -> none  [body(): lax.all_to_all(voltages, 'chan', split_axis=0, concat_axis=1, tiled=True)]
    all_to_all x0 -> x1, waiting for transfers between devices: none -> 11.9 us  [body(): lax.all_to_all(voltages, 'chan', split_axis=0, concat_axis=1, tiled=True)]
    transpose x3 -> x0, local copies, waits for them, and re-layouts: 6.36 us -> none  [the longest x1 3.48 us: body(): col_volts[0].reshape(tile_cols, TILE_SIDE, width).transpose(1, 0, 2)]
    all_to_all x0 -> x1, starting transfers between devices: none -> 6.32 us  [body(): lax.all_to_all(voltages, 'chan', split_axis=0, concat_axis=1, tiled=True)]
    unnamed x19 -> x17, local copies, waits for them, and re-layouts: 5.38 us -> 4.12 us
where the time goes in v3:
time: 239 us
  Pallas kernels  208 us (87%)
  waiting for transfers between devices  11.9 us (5%)
  local copies, waits for them, and re-layouts  10.8 us (5%)
  starting transfers between devices  6.32 us (3%)
    pallas_call x1, Pallas kernels, grid_tiles(): pl.pallas_call(functools.partial(grid_kernel, scale), grid=(steps,), in_s...  172 us
    pallas_call x1, Pallas kernels, gather_sides(): pl.pallas_call(functools.partial(gather_kernel, n_rows, n_cols), in_specs...  26.1 us
    all_to_all x1, waiting for transfers between devices, body(): lax.all_to_all(voltages, 'chan', split_axis=0, concat_axis=1, tiled=True)  11.9 us
    pallas_call x1, Pallas kernels, scatter_sum(): pl.pallas_call(functools.partial(scatter_kernel, n_rows, n_cols), in_spec...  10.2 us
    all_to_all x1, starting transfers between devices, body(): lax.all_to_all(voltages, 'chan', split_axis=0, concat_axis=1, tiled=True)  6.32 us
  transfers between devices with their start and end apart: 1, of which 1 were waited for; matrix products, arithmetic and copies ran while one was open for 1% of the time, Pallas kernels for 0%

profile of v3, /device:TPU:0, one launch (start us, length us, event | category | flops | bytes accessed | tf_op | source)
XLA Modules:
  0.0 239.1 jit_solution(7018836332859831363)
XLA Ops:
  0.0 6.3 %all-to-all-start = ((bf16[4,128,512]{2,1,0:T(8,128)(2,1)}), bf16[4,128,512]{2,1,0:T(8,128)(2,1)S(1)}, u32[]{:S(2)}, u32[]{:S(2)}) async-start(bf16[4,128,512]{2,1,0:T(8,128)(2,1)} %param.6), calls=%async_computation | async-start | bytes 1048576 | tf_op jit(solution)/shard_map/all_to_all | solution.py:285
  6.3 0.8 copy.58
  7.2 0.8 copy.41
  8.2 0.2 copy.73
  8.3 0.1 reshape.34
  8.6 0.1 copy.57
  8.7 0.1 reshape.32
  8.8 0.1 fusion.5.table_ref
  8.9 11.9 %all-to-all-done.own_ref = bf16[4,128,512]{2,1,0:T(8,128)(2,1)S(1)} async-done(((bf16[4,128,512]{2,1,0:T(8,128)(2,1)}), bf16[4,128,512]{2,1,0:T(8,128)(2,1)S(1)}, u32[]{:S(2)}, u32[]{:S(2)}) %all-to-all-start) | async-done | bytes 524320 | tf_op jit(solution)/shard_map/all_to_all | solution.py:285
  20.8 0.8 copy-done.3
  21.6 26.1 %shard_map.64 = (bf16[2,8,128,512]{3,2,1,0:T(8,128)(2,1)}, bf16[1,8,128,512]{3,2,1,0:T(8,128)(2,1)}) custom-call(bf16[4,128,512]{2,1,0:T(8,128)(2,1)} %copy-done.3), custom_call_target="tpu_custom_call" | custom-call | tf_op jit(solution)/shard_map/pallas_call | solution.py:262
  47.8 1.3 reshape_squeeze_reshape.6
  49.1 0.2 copy.39
  49.4 1.1 fusion.7
  50.4 2.5 %reshape_squeeze_reshape.7 = bf16[512,4,512]{2,1,0:T(4,128)(2,1)S(1)} reshape(bf16[2,8,128,512]{3,2,1,0:T(8,128)(2,1)} %get-tuple-element.8) | data formatting | bytes 4194304 | tf_op jit(solution)/shard_map/reshape;squeeze;reshape | solution.py:299
  53.0 1.7 copy.40
  54.8 0.2 maximum_maximum_fusion.left_ref
  55.0 0.8 copy-done
  55.8 0.2 copy-done.1
  56.0 0.2 copy-done.2
  56.1 171.9 %shard_map.65 = f32[512,256]{1,0:T(8,128)S(1)} custom-call(bf16[8,256,512]{2,1,0:T(8,128)(2,1)S(1)} %maximum_maximum_fusion.left_ref, bf16[2048,512]{1,0:T(8,128)(2,1)} %bitcast.88, s32[256,512]{1,0:T(8,128)S(1)} %bitcast.83, s32[256,512]{1,0:T(8,128)S(1)} %bitcast.84, s32[256,512]{1,0:T(8,128)S(1)} %bitcast.85, bf16[96,128]{1,0:T(8,128)(2,1)S(1)} %fusion.5.table_ref), custom_call_target="tpu_custom_call" | custom-call | tf_op jit(solution)/shard_map/pallas_call | solution.py:112
  228.0 0.2 copy.74
  228.2 10.2 %shard_map.66 = f32[1,2,32,256]{3,2,1,0:T(8,128)S(1)} custom-call(f32[1,2,256,256]{3,2,1,0:T(8,128)S(1)} %bitcast.82), custom_call_target="tpu_custom_call" | custom-call | tf_op jit(solution)/shard_map/pallas_call | solution.py:175
  238.4 0.6 copy.104
  (39 shorter events, 0.3 us)
Async XLA Ops:
  0.0 20.8 %all-to-all-start = ((bf16[4,128,512]{2,1,0:T(8,128)(2,1)}), bf16[4,128,512]{2,1,0:T(8,128)(2,1)S(1)}, u32[]{:S(2)}, u32[]{:S(2)}) async-start(bf16[4,128,512]{2,1,0:T(8,128)(2,1)} %param.6), calls=%async_computation | async-start | bytes 1048576 | tf_op jit(solution)/shard_map/all_to_all | solution.py:285
  20.8 0.8 copy-start.3
  53.0 1.8 copy-start.4
  53.0 1.8 copy-start.5
  54.8 1.0 copy-start
  54.8 1.2 copy-start.1
  54.8 1.4 copy-start.2
